TPU v7x, 512 devices: a whole 4x8x8 slice. The times are simulated.
512 devices in a mesh: kvp: 64 (over z, y), head: 8 (over x, core).
Axes of the slice: x: 4, y: 8, z: 8, core: 2. Of those that a mesh axis runs over, the one named last changes fastest.
Arguments:
- stream_in: bfloat16 [8, 16384], P(None, 'kvp'), may hold values from -64 to 64
- queries: bfloat16 [8, 8, 16, 128], P(None, 'head'), may hold values from -16 to 16
- key_cache: bfloat16 [8, 8, 8192, 128], P(None, 'head', 'kvp'), may hold values from -40 to 40
- value_cache: bfloat16 [8, 8, 8192, 128], P(None, 'head', 'kvp'), may hold values from -384 to 384
- lengths: int32 [8], replicated, may hold values from 1024 to 8192, as said below
- out_weight: bfloat16 [16384, 16384], P('head', 'kvp'), may hold values from -0.046875 to 0.046875
- norm_gain: bfloat16 [16384], P('kvp'), may hold values from 0.099609375 to 1.8984375
- gate_weight: bfloat16 [16384, 26624], P('kvp', 'head'), may hold values from -0.046875 to 0.046875
- up_weight: bfloat16 [16384, 26624], P('kvp', 'head'), may hold values from -0.046875 to 0.046875
Outputs:
- stream_out: bfloat16 [8, 16384], P(None, ('kvp', 'head'))
- hidden: bfloat16 [8, 26624], P(None, 'head')
Inputs may be any that keep to these rules, and one draw needn't show every extreme that they name: `lengths`: some session has exactly 8192 filled positions and some exactly 1024.
All inputs are finite; a program needn't handle non-finite values.
Results may differ from a plain program's by a relative error of at most 0.02.
Values may be sent and summed in bfloat16 or wider, within the bound.
A program may use at most 64 MiB of HBM per device.

v0:
```python
import jax
import jax.numpy as jnp
from jax import lax
from jax.sharding import PartitionSpec as P

D = 16384


neg_fill = -1e30
epsilon = 1e-05


def body(
    stream_in,
    queries,
    key_cache,
    value_cache,
    lengths,
    out_weight,
    norm_gain,
    gate_weight,
    up_weight,
):
    sessions = queries.shape[0]
    head_dim = queries.shape[3]
    pos_local = key_cache.shape[2]
    offset = lax.axis_index("kvp") * pos_local
    positions = offset + lax.iota(jnp.int32, pos_local)
    included = positions[None, None, :] < lengths[:, None, None]
    query_rows = queries[:, 0]
    key_block = key_cache[:, 0]
    value_block = value_cache[:, 0].astype(jnp.float32)
    scores = jnp.einsum(
        "sjd,spd->sjp", query_rows, key_block, preferred_element_type=jnp.float32
    ) * head_dim ** (-0.5)
    scores = jnp.where(included, scores, neg_fill)
    local_max = jnp.max(scores, axis=2)
    top_score = lax.pmax(local_max, "kvp")
    weights = jnp.where(included, jnp.exp(scores - top_score[:, :, None]), 0.0)
    weight_sum = jnp.sum(weights, axis=2)
    weighted = jnp.einsum("sjp,spd->sjd", weights, value_block)
    weight_sum, weighted = lax.psum((weight_sum, weighted), "kvp")
    attended = (weighted / weight_sum[:, :, None]).astype(jnp.bfloat16).reshape(sessions, -1)
    partial_value = jnp.dot(attended, out_weight, preferred_element_type=jnp.float32)
    head_count = lax.axis_size("head")
    projected = lax.psum(partial_value, "head")
    residual_new = (stream_in.astype(jnp.float32) + projected).astype(jnp.bfloat16)
    widened = residual_new.astype(jnp.float32)
    square_sum = lax.psum(jnp.sum(widened * widened, axis=1), "kvp")
    inverse = lax.rsqrt(square_sum / D + epsilon)
    normed = (widened * inverse[:, None] * norm_gain.astype(jnp.float32)).astype(jnp.bfloat16)
    share_width = residual_new.shape[1] // head_count
    stream_out = lax.dynamic_slice_in_dim(
        residual_new, lax.axis_index("head") * share_width, share_width, 1
    )
    gate_part = jnp.dot(normed, gate_weight, preferred_element_type=jnp.float32)
    up_part = jnp.dot(normed, up_weight, preferred_element_type=jnp.float32)
    gate_full, up_full = lax.psum((gate_part, up_part), "kvp")
    hidden = (jax.nn.silu(gate_full) * up_full).astype(jnp.bfloat16)
    return (stream_out, hidden)


def solution(mesh):
    return jax.shard_map(
        body,
        mesh=mesh,
        in_specs=(
            P(None, "kvp"),
            P(None, "head", None, None),
            P(None, "head", "kvp", None),
            P(None, "head", "kvp", None),
            P(),
            P("head", "kvp"),
            P("kvp"),
            P("kvp", "head"),
            P("kvp", "head"),
        ),
        out_specs=(P(None, ("kvp", "head")), P(None, "head")),
        check_vma=False,
    )
```

profile of v0, /device:TPU:2, one launch (start us, length us, event | category | flops | bytes accessed | tf_op | source)
XLA Modules:
  0.0 610.7 jit_solution(14653483641606383077)
XLA Ops:
  7.2 0.0 copy-start
  7.2 0.0 copy-start.2
  7.2 0.0 all-reduce.4.cloned.1.call-start
  7.3 0.8 broadcast_compare_fusion
  8.1 1.3 fusion.21
  9.4 149.9 %pmax.7 = f32[8,16]{1,0:T(8,128)S(1)} all-reduce(f32[8,16]{1,0:T(8,128)S(1)} %get-tuple-element.6), channel_id=1, replica_groups=mesh['kvp'=64,'head'=8] {'kvp'}, use_global_device_ids=true, to_apply=%region_1.2 | all-reduce | flops 128 | bytes 1024 | tf_op jit(solution)/shard_map/pmax | solution.py:38
  159.3 0.0 copy-start.1
  159.3 1.9 fusion.1
  161.2 0.0 all-reduce.4.cloned.1.call-update
  161.2 0.0 all-reduce.6.cloned.1.call-start
  161.3 0.7 convert_element_type.26
  162.0 0.2 fusion.4
  162.1 138.0 %psum.43 = f32[8,16]{1,0:T(8,128)S(1)} all-reduce(f32[8,16]{1,0:T(8,128)S(1)} %fusion.4), channel_id=1, replica_groups=mesh['kvp'=64,'head'=8] {'kvp'}, use_global_device_ids=true, to_apply=%region_4.5 | all-reduce | flops 128 | bytes 1024 | tf_op jit(solution)/shard_map/psum | solution.py:42
  300.1 1.1 all-reduce.4.cloned.1.call-done
  301.2 0.9 fusion.11
  302.2 1.5 fusion.5
  303.6 10.2 %psum.44 = f32[8,256]{1,0:T(8,128)S(1)} all-reduce(f32[8,256]{1,0:T(8,128)S(1)} %fusion.5), channel_id=1, replica_groups=mesh['kvp'=64,'head'=8] {'head'}, use_global_device_ids=true, to_apply=%region_5.6 | all-reduce | flops 2048 | bytes 16384 | tf_op jit(solution)/shard_map/psum | solution.py:46
  313.9 0.0 copy-done.2
  313.9 0.1 fusion.13
  314.0 140.0 %psum.45 = f32[8]{0:T(128)S(1)} all-reduce(f32[8]{0:T(128)S(1)} %get-tuple-element.4), channel_id=1, replica_groups=mesh['kvp'=64,'head'=8] {'kvp'}, use_global_device_ids=true, to_apply=%region_7.8 | all-reduce | flops 8 | bytes 64 | tf_op jit(solution)/shard_map/psum | solution.py:49
  454.0 0.0 copy-done
  454.0 1.0 fusion.16
  455.1 0.0 copy-done.1
  455.1 1.0 fusion.18
  456.1 0.0 all-reduce.6.cloned.1.call-update
  456.1 0.7 constant_dynamic-slice_fusion
  456.8 145.5 %all-reduce.6.cloned.1.call-done = (f32[8,3328]{1,0:T(8,128)}, f32[8,3328]{1,0:T(8,128)}) async-done(((f32[8,3328]{1,0:T(8,128)}, f32[8,3328]{1,0:T(8,128)}), (f32[8,3328]{1,0:T(8,128)}, f32[8,3328]{1,0:T(8,128)})) %all-reduce.6.cloned.1.call-update) | async-done | bytes 213008 | tf_op jit(solution)/shard_map/psum | solution.py:58
  602.3 1.6 multiply_convert_fusion
  (2 shorter events, 0.0 us)
Async XLA Ops:
  7.2 446.9 %copy-start = (bf16[256,3328]{1,0:T(8,128)(2,1)S(1)}, bf16[256,3328]{1,0:T(8,128)(2,1)}, u32[]{:S(2)}) copy-start(bf16[256,3328]{1,0:T(8,128)(2,1)} %param.17) | copy-start | bytes 5111812
  7.2 306.7 %copy-start.2 = (bf16[8,256]{1,0:T(8,128)(2,1)S(1)}, bf16[8,256]{1,0:T(8,128)(2,1)}, u32[]{:S(2)}) copy-start(bf16[8,256]{1,0:T(8,128)(2,1)} %param.9) | copy-start | bytes 12292
  7.2 294.1 %all-reduce.4.cloned.1.call-start = ((), (), s32[]{:S(2)}) async-start(), calls=%async_computation | async-start | bytes 131072 | tf_op jit(solution)/shard_map/psum | solution.py:42
  159.3 295.8 %copy-start.1 = (bf16[256,3328]{1,0:T(8,128)(2,1)S(1)}, bf16[256,3328]{1,0:T(8,128)(2,1)}, u32[]{:S(2)}) copy-start(bf16[256,3328]{1,0:T(8,128)(2,1)} %param.16) | copy-start | bytes 5111812
  161.2 441.1 %all-reduce.6.cloned.1.call-start = ((), (), s32[]{:S(2)}) async-start(), calls=%async_computation.1 | async-start | bytes 425984 | tf_op jit(solution)/shard_map/psum | solution.py:58
Sparse Core Ops, SparseCore 0:
  161.4 139.8 all-reduce.3
  456.2 146.0 all-reduce.5
where the time goes:
time: 611 us
  blocking collectives  438 us (72%)
  waiting for transfers between devices  147 us (24%)
  between operations  14.1 us (2%)
  matrix products  6.73 us (1%)
    pmax x1, blocking collectives, body(): top_score = lax.pmax(local_max, 'kvp')  150 us
    psum x1, waiting for transfers between devices, body(): gate_full, up_full = lax.psum((gate_part, up_part), 'kvp')  146 us
    psum x1, blocking collectives, body(): square_sum = lax.psum(jnp.sum(widened * widened, axis=1), 'kvp')  140 us
    psum x1, blocking collectives, body(): weight_sum, weighted = lax.psum((weight_sum, weighted), 'kvp')  138 us
  transfers between devices with their start and end apart: 2, of which 2 were waited for; matrix products, arithmetic and copies ran while one was open for 0% of the time, Pallas kernels for 0%

commit v1 on v0

v1 whole, which is shorter than its diff:
```python
import jax
import jax.numpy as jnp
from jax import lax
from jax.experimental import pallas as pl
from jax.experimental.pallas import tpu as pltpu
from jax.sharding import PartitionSpec as P

D = 16384
neg_fill = -1e30
epsilon = 1e-05
MESH = pl.DeviceIdType.MESH
FAR_FIRST = (4, 3, 5, 2, 6, 1, 7)
F32 = jnp.float32
BF16 = jnp.bfloat16


def merge(parts, axis):
    total = parts[:, 0:8, :]
    stats = parts[:, 8:16, :]
    turned = jnp.concatenate([stats[:, :, 64:], stats[:, :, :64]], axis=2)
    low = lax.broadcasted_iota(jnp.int32, stats.shape, 2) < 64
    shift = jnp.where(low, stats, turned)
    weight = jnp.where(low, turned, stats)
    top = jnp.max(shift, axis=0)
    scale = jnp.exp(shift - top[None])
    return jnp.sum(scale * total, axis=0), top, jnp.sum(scale * weight, axis=0)


def pack_stats(total, top, weight):
    low = lax.broadcasted_iota(jnp.int32, top.shape, 1) < 64
    return jnp.concatenate([total, jnp.where(low, top, weight)], axis=0).astype(BF16)


def kernel(
    stream_hbm, q_hbm, k_hbm, v_hbm, len_hbm, ow_hbm, gain_hbm, gw_hbm, uw_hbm,
    so_ref, hid_ref,
    stream_ref, q_ref, k_ref, v_ref, len_ref, ow_ref, gain_ref, gw_ref, uw_ref, in_sem,
    a1_send, a1_recv, a2_send, a2_recv, a3_send, a3_recv,
    h_send, h_recv, d1_send, d1_recv, d2_send, d2_recv, d3_send, d3_recv,
    send_sem, recv_sem,
):
    kvp, head = lax.axis_index("kvp"), lax.axis_index("head")
    z, y = kvp // 8, lax.rem(kvp, 8)

    def at_z(p):
        return (p * 8 + y, head)

    def at_y(p):
        return (z * 8 + p, head)

    def at_head(p):
        return (kvp, p)

    axes = ((z, at_z), (y, at_y))

    barrier = pltpu.get_barrier_semaphore()
    for me, at in axes + ((head, at_head),):
        for d in FAR_FIRST:
            pl.semaphore_signal(barrier, inc=1, device_id=at(lax.rem(me + d, 8)), device_id_type=MESH)

    loads = {}
    for n, (name, src, dst) in enumerate((
        ("len", len_hbm, len_ref), ("q", q_hbm, q_ref), ("k", k_hbm, k_ref), ("v", v_hbm, v_ref),
        ("stream", stream_hbm, stream_ref), ("gain", gain_hbm, gain_ref),
        ("ow", ow_hbm, ow_ref), ("gw", gw_hbm, gw_ref), ("uw", uw_hbm, uw_ref),
    )):
        loads[name] = pltpu.make_async_copy(src, dst, in_sem.at[n])
        loads[name].start()

    def send(phase, axis, src_of, recv):
        me, at = axis
        for d in FAR_FIRST:
            p = lax.rem(me + d, 8)
            pltpu.make_async_remote_copy(
                src_of(p), recv.at[me], send_sem.at[phase], recv_sem.at[phase], device_id=at(p), device_id_type=MESH
            ).start()

    def arrived(phase, recv):
        seven = recv.at[pl.ds(0, 7)]
        pltpu.make_async_copy(seven, seven, recv_sem.at[phase]).wait()

    for name in ("len", "q", "k", "v"):
        loads[name].wait()
    lane = lax.broadcasted_iota(jnp.int32, (16, 128), 1)
    position = kvp * 128 + lane
    low = lane < 64
    for s in range(8):
        score = lax.dot_general(
            q_ref[s], k_ref[s], (((1,), (1,)), ((), ())), preferred_element_type=F32
        ) * (128**-0.5)
        inside = position < len_ref[s]
        score = jnp.where(inside, score, neg_fill)
        top = jnp.max(score, axis=1, keepdims=True).astype(BF16).astype(F32)
        weight = jnp.where(inside, jnp.exp(score - top), 0.0).astype(BF16)
        weight_sum = jnp.sum(weight.astype(F32), axis=1, keepdims=True)
        total = jnp.dot(weight, v_ref[s], preferred_element_type=F32)
        stats = jnp.where(low, top, weight_sum)
        for j in range(2):
            rows = slice(8 * j, 8 * j + 8)
            a1_send[s // 4, (s % 4) * 2 + j] = jnp.concatenate([total[rows], stats[rows]], axis=0).astype(BF16)

    pl.semaphore_wait(barrier, 21)
    for f in range(2):
        send(f, axes[f], lambda p: a1_send.at[f, p], a1_recv.at[f])
        me = axes[f][0]
        a1_recv[f, me] = a1_send[f, me]
    for f in range(2):
        arrived(f, a1_recv.at[f])
        a2_send[f] = pack_stats(*merge(a1_recv[f].astype(F32), f))
        send(2 + f, axes[1 - f], lambda p: a2_send.at[f], a2_recv.at[f])
        a2_recv[f, axes[1 - f][0]] = a2_send[f]
    for f in range(2):
        arrived(2 + f, a2_recv.at[f])
        total, _, weight = merge(a2_recv[f].astype(F32), f)
        a3_send[f] = (total / weight).astype(BF16).astype(F32)
        send(4 + f, axes[f], lambda p: a3_send.at[f], a3_recv.at[pl.ds(8 * f, 8)])
        a3_recv[8 * f + axes[f][0]] = a3_send[f]
    for f in range(2):
        arrived(4 + f, a3_recv.at[pl.ds(8 * f, 8)])

    loads["ow"].wait()
    loads["stream"].wait()
    loads["gain"].wait()
    rows = a3_recv[...].reshape(8, 16, 128)
    attended = jnp.concatenate([rows[:, j, :] for j in range(16)], axis=1).astype(BF16)
    h_send[...] = jnp.dot(attended, ow_ref[...], preferred_element_type=F32)
    send(6, (head, at_head), lambda p: h_send, h_recv)
    h_recv[head] = h_send[...]
    arrived(6, h_recv)
    projected = jnp.sum(h_recv[...], axis=0)
    stream_out = (stream_ref[...].astype(F32) + projected).astype(BF16)
    so_ref[...] = stream_out
    widened = stream_out.astype(F32)
    square = jnp.broadcast_to(jnp.sum(widened * widened, axis=1, keepdims=True), (8, 128))
    scaled = (widened * gain_ref[...].astype(F32)).astype(BF16)

    loads["gw"].wait()
    loads["uw"].wait()
    high = square.astype(BF16)
    squares = jnp.concatenate([square, square - high.astype(F32)], axis=0).astype(BF16)

    def eighth(f, k):
        columns = pl.ds(pl.multiple_of((13 * f + (13 * k) // 8) * 128, 128), 256)
        gate = jnp.dot(scaled, gw_ref[:, columns], preferred_element_type=F32)
        up = jnp.dot(scaled, uw_ref[:, columns], preferred_element_type=F32)
        return jnp.concatenate([jnp.concatenate([gate, up], axis=0).astype(BF16), squares], axis=1)

    for d in FAR_FIRST:
        for f in range(2):
            me, at = axes[f]
            p = lax.rem(me + d, 8)
            d1_send[f, p] = eighth(f, p)
            pltpu.make_async_remote_copy(
                d1_send.at[f, p], d1_recv.at[f, me], send_sem.at[7 + f], recv_sem.at[7 + f],
                device_id=at(p), device_id_type=MESH,
            ).start()
    for f in range(2):
        me = axes[f][0]
        d1_recv[f, me] = eighth(f, me)
    for f in range(2):
        arrived(7 + f, d1_recv.at[f])
        part = jnp.sum(d1_recv[f].astype(F32), axis=0)
        square = part[0:8, 256:] + part[8:16, 256:]
        rest = square - square.astype(BF16).astype(F32)
        part = jnp.concatenate([part[:, :256], jnp.concatenate([square, rest], axis=0)], axis=1)
        d2_send[f] = part.astype(BF16)
        send(9 + f, axes[1 - f], lambda p: d2_send.at[f], d2_recv.at[f])
        d2_recv[f, axes[1 - f][0]] = d2_send[f]
    for f in range(2):
        arrived(9 + f, d2_recv.at[f])
        part = jnp.sum(d2_recv[f].astype(F32), axis=0)
        square = part[0:8, 256:] + part[8:16, 256:]
        inverse = lax.rsqrt(square / D + epsilon)
        inverse = jnp.concatenate([inverse, inverse], axis=1)
        gate, up = part[0:8, :256] * inverse, part[8:16, :256] * inverse
        hidden = gate / (1.0 + jnp.exp(-gate)) * up
        d3_send[f] = jnp.concatenate([hidden[:, :128], hidden[:, 128:]], axis=0).astype(BF16)
        send(11 + f, axes[f], lambda p: d3_send.at[f], d3_recv.at[f])
        d3_recv[f, axes[f][0]] = d3_send[f]
    for f in range(2):
        arrived(11 + f, d3_recv.at[f])
        for t in range(13):
            k = max(k for k in range(8) if 13 * k // 8 <= t)
            half = t - 13 * k // 8
            hid_ref[:, (13 * f + t) * 128 : (13 * f + t + 1) * 128] = d3_recv[f, k, 8 * half : 8 * half + 8, :]

    for f in range(2):
        for phase, buffer in (
            (f, a1_send.at[f, pl.ds(0, 7)]),
            (2 + f, a1_send.at[f, pl.ds(0, 7)]),
            (4 + f, a3_recv.at[pl.ds(0, 7)]),
            (7 + f, d1_send.at[f, pl.ds(0, 7)]),
            (9 + f, d1_send.at[f, pl.ds(0, 7)]),
            (11 + f, d3_recv.at[f, pl.ds(0, 7)]),
        ):
            pltpu.make_async_copy(buffer, buffer, send_sem.at[phase]).wait()
    seven = h_recv.at[pl.ds(0, 7)]
    pltpu.make_async_copy(seven, seven, send_sem.at[6]).wait()


def body(stream_in, queries, key_cache, value_cache, lengths, out_weight, norm_gain, gate_weight, up_weight):
    vmem, dma = pltpu.VMEM, pltpu.SemaphoreType.DMA
    residual, hidden = pl.pallas_call(
        kernel,
        out_shape=(jax.ShapeDtypeStruct((8, 256), BF16), jax.ShapeDtypeStruct((8, 3328), BF16)),
        in_specs=[pl.BlockSpec(memory_space=pl.ANY)] * 9,
        out_specs=(pl.BlockSpec(memory_space=vmem), pl.BlockSpec(memory_space=vmem)),
        scratch_shapes=[
            vmem((8, 256), BF16),
            vmem((8, 16, 128), BF16),
            vmem((8, 128, 128), BF16),
            vmem((8, 128, 128), BF16),
            pltpu.SMEM((8,), jnp.int32),
            vmem((2048, 256), BF16),
            vmem((1, 256), BF16),
            vmem((256, 3328), BF16),
            vmem((256, 3328), BF16),
            dma((9,)),
            vmem((2, 8, 16, 128), BF16),
            vmem((2, 8, 16, 128), BF16),
            vmem((2, 16, 128), BF16),
            vmem((2, 8, 16, 128), BF16),
            vmem((2, 8, 128), F32),
            vmem((16, 8, 128), F32),
            vmem((8, 256), F32),
            vmem((8, 8, 256), F32),
            vmem((2, 8, 16, 384), BF16),
            vmem((2, 8, 16, 384), BF16),
            vmem((2, 16, 384), BF16),
            vmem((2, 8, 16, 384), BF16),
            vmem((2, 16, 128), BF16),
            vmem((2, 8, 16, 128), BF16),
            dma((13,)),
            dma((13,)),
        ],
        compiler_params=pltpu.CompilerParams(
            collective_id=0, has_side_effects=True, vmem_limit_bytes=60 * 1024 * 1024
        ),
        name="decode_step",
    )(
        stream_in, queries[:, 0], key_cache[:, 0], value_cache[:, 0], lengths, out_weight,
        norm_gain.reshape(1, 256), gate_weight, up_weight,
    )
    stream_out = lax.dynamic_slice_in_dim(residual, lax.axis_index("head") * 32, 32, 1)
    return stream_out, hidden


def solution(mesh):
    return jax.shard_map(
        body,
        mesh=mesh,
        in_specs=(
            P(None, "kvp"),
            P(None, "head", None, None),
            P(None, "head", "kvp", None),
            P(None, "head", "kvp", None),
            P(),
            P("head", "kvp"),
            P("kvp"),
            P("kvp", "head"),
            P("kvp", "head"),
        ),
        out_specs=(P(None, ("kvp", "head")), P(None, "head")),
        check_vma=False,
    )
```

time: 611 us -> 53.2 us (0.09)
  the two profiles are of different devices: /device:TPU:2 before, /device:TPU:8 now
where the time goes in v1:
time: 53.2 us; the launch traced here: 53 us
  Pallas kernels  48.4 us (91%)
  local copies, waits for them, and re-layouts  3.98 us (7%)
  between operations  0.64 us (1%)
    pallas_call x1, Pallas kernels, body(): pl.pallas_call(kernel, out_shape=(jax.ShapeDtypeStruct((8, 256), BF16), j...  48.4 us
    unnamed x1, local copies, waits for them, and re-layouts  1.43 us
    dynamic_slice x1, local copies, waits for them, and re-layouts, body(): lax.dynamic_slice_in_dim(residual, lax.axis_index('head') * 32, 32, 1)  1.32 us
    reshape x1, local copies, waits for them, and re-layouts, body(): norm_gain.reshape(1, 256)  1.22 us

profile of v1, /device:TPU:8, one launch (start us, length us, event | category | flops | bytes accessed | tf_op | source)
XLA Modules:
  0.0 53.0 jit_solution(16361268456599229004)
XLA Ops:
  0.6 1.2 %reshape.7.gain_hbm = bf16[1,256]{1,0:T(2,128)(2,1)} reshape(bf16[256]{0:T(256)(128)(2,1)} %param.15) | data formatting | bytes 1024 | tf_op jit(solution)/shard_map/reshape | solution.py:242
  1.9 48.4 %decode_step.1 = (bf16[8,256]{1,0:T(8,128)(2,1)}, bf16[8,3328]{1,0:T(8,128)(2,1)}) custom-call(bf16[8,256]{1,0:T(8,128)(2,1)} %stream_hbm.1, bf16[8,16,128]{2,1,0:T(8,128)(2,1)} %bitcast.5, bf16[8,128,128]{2,1,0:T(8,128)(2,1)} %bitcast.3, bf16[8,128,128]{2,1,0:T(8,128)(2,1)} %bitcast.4, s32[8]{0:T(128)} %len_hbm.1, bf16[2048,256]{1,0:T(8,128)(2,1)} %ow_hbm.1, ...), custom_call_target="tpu_custom_call" | custom-call | tf_op jit(solution)/shard_map/decode_step/pallas_call | solution.py:203
  50.3 1.3 %constant_dynamic-slice_fusion = bf16[8,32]{1,0:T(8,128)(2,1)} fusion(bf16[8,256]{1,0:T(8,128)(2,1)} %get-tuple-element.4, s32[]{:T(128)S(6)} %select_n.3), kind=kLoop, calls=%fused_computation | loop fusion | bytes 1028 | tf_op jit(solution)/shard_map/dynamic_slice | solution.py:244
  51.6 1.4 %copy.12 = bf16[8,3328]{1,0:T(8,128)(2,1)} copy(bf16[8,3328]{1,0:T(8,128)(2,1)} %get-tuple-element.9) | data formatting | bytes 106496

commit v2 on v1

v2 whole, which is shorter than its diff:
```python
import jax
import jax.numpy as jnp
from jax import lax
from jax.experimental import pallas as pl
from jax.experimental.pallas import tpu as pltpu
from jax.sharding import PartitionSpec as P

D = 16384
neg_fill = -1e30
epsilon = 1e-05
MESH = pl.DeviceIdType.MESH
F32 = jnp.float32
BF16 = jnp.bfloat16


def merge(parts):
    stats = parts[:, 64:80, :].astype(F32)
    shift = jnp.max(stats, axis=0)
    scale = jnp.exp(stats - shift[None])
    weight = jnp.sum(scale * pltpu.roll(stats.reshape(128, 128), 112, 1).reshape(8, 16, 128), axis=0)
    totals = []
    for s in range(4):
        total = None
        for k in range(8):
            term = scale[k, :, 32 * s : 32 * s + 1] * parts[k, 16 * s : 16 * s + 16, :].astype(F32)
            total = term if total is None else total + term
        totals.append(total)
    return totals, shift, weight


def kernel(
    stream_hbm, q_hbm, k_hbm, v_hbm, len_hbm, ow_hbm, gain_hbm, gw_hbm, uw_hbm,
    so_ref, hid_ref,
    stream_ref, q_ref, k_ref, v_ref, len_ref, ow_ref, gain_ref, gw_ref, uw_ref, in_sem,
    a1_send, a1_recv, a2_send, a2_recv, rows,
    h_send, h_recv, d1_send, d1_recv, d2_send, d2_recv, d3_send, d3_recv,
    send_sem, recv_sem,
):
    kvp, head = lax.axis_index("kvp"), lax.axis_index("head")
    z, y = kvp // 8, lax.rem(kvp, 8)

    def at_z(p):
        return (p * 8 + y, head)

    def at_y(p):
        return (z * 8 + p, head)

    def at_head(p):
        return (kvp, p)

    def place(f):
        return jnp.where(f == 0, z, y)

    def at(f, p):
        return (jnp.where(f == 0, p * 8 + y, z * 8 + p), head)

    def far_first(me, n):
        half = (n + 1) // 2
        return lax.rem(me + jnp.where(lax.rem(n, 2) == 0, 4 + half, 4 - half), 8)

    barrier = pltpu.get_barrier_semaphore()

    @pl.loop(0, 7)
    def _(n):
        for target in (at_z(far_first(z, n)), at_y(far_first(y, n)), at_head(far_first(head, n))):
            pl.semaphore_signal(barrier, inc=1, device_id=target, device_id_type=MESH)

    loads = {}
    for n, (name, src, dst) in enumerate((
        ("len", len_hbm, len_ref), ("q", q_hbm, q_ref), ("k", k_hbm, k_ref), ("v", v_hbm, v_ref),
        ("stream", stream_hbm, stream_ref), ("gain", gain_hbm, gain_ref),
        ("ow", ow_hbm, ow_ref), ("gw", gw_hbm, gw_ref), ("uw", uw_hbm, uw_ref),
    )):
        loads[name] = pltpu.make_async_copy(src, dst, in_sem.at[n])
        loads[name].start()

    def send(phase, f, src_of, recv):
        me = place(f)

        @pl.loop(0, 7)
        def _(n):
            p = far_first(me, n)
            pltpu.make_async_remote_copy(
                src_of(p), recv.at[me], send_sem.at[phase], recv_sem.at[phase], device_id=at(f, p), device_id_type=MESH
            ).start()

    def arrived(phase, recv):
        seven = recv.at[pl.ds(0, 7)]
        pltpu.make_async_copy(seven, seven, recv_sem.at[phase]).wait()

    for name in ("len", "q", "k", "v"):
        loads[name].wait()
    lane = lax.broadcasted_iota(jnp.int32, (16, 128), 1)
    position = kvp * 128 + lane
    for f in range(2):
        stats = jnp.zeros((16, 128), F32)
        for s in range(4):
            score = lax.dot_general(
                q_ref[4 * f + s], k_ref[4 * f + s], (((1,), (1,)), ((), ())), preferred_element_type=F32
            ) * (128**-0.5)
            inside = position < len_ref[4 * f + s]
            score = jnp.where(inside, score, neg_fill)
            top = jnp.max(score, axis=1, keepdims=True).astype(BF16).astype(F32)
            weight = jnp.where(inside, jnp.exp(score - top), 0.0).astype(BF16)
            weight_sum = jnp.sum(weight.astype(F32), axis=1, keepdims=True)
            total = jnp.dot(weight, v_ref[4 * f + s], preferred_element_type=F32)
            a1_send[f, 16 * s : 16 * s + 16] = total.astype(BF16)
            stats = jnp.where(lane // 16 == 2 * s, top, jnp.where(lane // 16 == 2 * s + 1, weight_sum, stats))
        a1_send[f, 64:80] = stats.astype(BF16)

    pl.semaphore_wait(barrier, 21)

    @pl.loop(0, 2)
    def _(f):
        send(f, f, lambda p: a1_send.at[f], a1_recv.at[f])
        a1_recv[f, place(f)] = a1_send[f]


    @pl.loop(0, 2)
    def _(f):
        arrived(f, a1_recv.at[f])
        totals, shift, weight = merge(a1_recv[f])
        for s in range(4):
            a2_send[f, 16 * s : 16 * s + 16] = totals[s].astype(BF16)
        a2_send[f, 64:80] = jnp.where(lax.rem(lane // 16, 2) == 0, shift, pltpu.roll(weight, 16, 1)).astype(BF16)
        send(2 + f, 1 - f, lambda p: a2_send.at[f], a2_recv.at[f])
        a2_recv[f, place(1 - f)] = a2_send[f]

    @pl.loop(0, 2)
    def _(f):
        arrived(2 + f, a2_recv.at[f])
        totals, _, weight = merge(a2_recv[f])
        inverse = 1.0 / weight
        for s in range(4):
            rows[pl.ds(64 * f + 16 * s, 16)] = totals[s] * inverse[:, 32 * s : 32 * s + 1]

    loads["ow"].wait()
    loads["stream"].wait()
    loads["gain"].wait()
    attended = jnp.concatenate([rows[pl.ds(j, 8, stride=16), :] for j in range(16)], axis=1).astype(BF16)
    h_send[...] = jnp.dot(attended, ow_ref[...], preferred_element_type=F32)

    @pl.loop(0, 7)
    def _(n):
        p = far_first(head, n)
        pltpu.make_async_remote_copy(
            h_send, h_recv.at[head], send_sem.at[6], recv_sem.at[6], device_id=at_head(p), device_id_type=MESH
        ).start()

    h_recv[head] = h_send[...]
    arrived(6, h_recv)
    projected = jnp.sum(h_recv[...], axis=0)
    stream_out = (stream_ref[...].astype(F32) + projected).astype(BF16)
    so_ref[...] = stream_out
    widened = stream_out.astype(F32)
    square = jnp.broadcast_to(jnp.sum(widened * widened, axis=1, keepdims=True), (8, 128))
    scaled = (widened * gain_ref[...].astype(F32).reshape(1, 256)).astype(BF16)

    loads["gw"].wait()
    loads["uw"].wait()
    high = square.astype(BF16)
    squares = jnp.concatenate([square, square - high.astype(F32)], axis=0).astype(BF16)

    def eighth(f, k):
        columns = pl.ds(pl.multiple_of((13 * f + (13 * k) // 8) * 128, 128), 256)
        gate = jnp.dot(scaled, gw_ref[:, columns], preferred_element_type=F32)
        up = jnp.dot(scaled, uw_ref[:, columns], preferred_element_type=F32)
        return jnp.concatenate([jnp.concatenate([gate, up], axis=0).astype(BF16), squares], axis=1)

    @pl.loop(0, 8)
    def _(n):
        for f in range(2):
            me = place(f)
            p = far_first(me, n)
            d1_send[f, p] = eighth(f, p)

            @pl.when(n < 7)
            def _():
                pltpu.make_async_remote_copy(
                    d1_send.at[f, p], d1_recv.at[f, me], send_sem.at[7 + f], recv_sem.at[7 + f],
                    device_id=at(f, p), device_id_type=MESH,
                ).start()

    @pl.loop(0, 2)
    def _(f):
        d1_recv[f, place(f)] = d1_send[f, place(f)]
        arrived(7 + f, d1_recv.at[f])
        part = jnp.sum(d1_recv[f].astype(F32), axis=0)
        square = part[0:8, 256:] + part[8:16, 256:]
        rest = square - square.astype(BF16).astype(F32)
        part = jnp.concatenate([part[:, :256], jnp.concatenate([square, rest], axis=0)], axis=1)
        d2_send[f] = part.astype(BF16)
        send(9 + f, 1 - f, lambda p: d2_send.at[f], d2_recv.at[f])
        d2_recv[f, place(1 - f)] = d2_send[f]

    @pl.loop(0, 2)
    def _(f):
        arrived(9 + f, d2_recv.at[f])
        part = jnp.sum(d2_recv[f].astype(F32), axis=0)
        square = part[0:8, 256:] + part[8:16, 256:]
        inverse = lax.rsqrt(square / D + epsilon)
        inverse = jnp.concatenate([inverse, inverse], axis=1)
        gate, up = part[0:8, :256] * inverse, part[8:16, :256] * inverse
        hidden = gate / (1.0 + jnp.exp(-gate)) * up
        d3_send[f] = jnp.concatenate([hidden[:, :128], hidden[:, 128:]], axis=0).astype(BF16)
        send(11 + f, f, lambda p: d3_send.at[f], d3_recv.at[f])
        d3_recv[f, place(f)] = d3_send[f]

    for f in range(2):
        arrived(11 + f, d3_recv.at[f])
        for t in range(13):
            k = max(k for k in range(8) if 13 * k // 8 <= t)
            half = t - 13 * k // 8
            hid_ref[:, (13 * f + t) * 128 : (13 * f + t + 1) * 128] = d3_recv[f, k, 8 * half : 8 * half + 8, :]

    for f in range(2):
        for phase, buffer in (
            (f, a1_recv.at[f, pl.ds(0, 7)]),
            (2 + f, a2_recv.at[f, pl.ds(0, 7)]),
            (7 + f, d1_send.at[f, pl.ds(0, 7)]),
            (9 + f, d1_send.at[f, pl.ds(0, 7)]),
            (11 + f, d3_recv.at[f, pl.ds(0, 7)]),
        ):
            pltpu.make_async_copy(buffer, buffer, send_sem.at[phase]).wait()
    seven = h_recv.at[pl.ds(0, 7)]
    pltpu.make_async_copy(seven, seven, send_sem.at[6]).wait()


def body(stream_in, queries, key_cache, value_cache, lengths, out_weight, norm_gain, gate_weight, up_weight):
    vmem, dma = pltpu.VMEM, pltpu.SemaphoreType.DMA
    residual, hidden = pl.pallas_call(
        kernel,
        out_shape=(vmem((8, 256), BF16), vmem((8, 3328), BF16)),
        in_specs=[pl.BlockSpec(memory_space=pl.ANY)] * 9,
        out_specs=(pl.BlockSpec(memory_space=vmem), pl.BlockSpec(memory_space=vmem)),
        scratch_shapes=[
            vmem((8, 256), BF16),
            vmem((8, 16, 128), BF16),
            vmem((8, 128, 128), BF16),
            vmem((8, 128, 128), BF16),
            pltpu.SMEM((8,), jnp.int32),
            vmem((2048, 256), BF16),
            vmem((256,), BF16),
            vmem((256, 3328), BF16),
            vmem((256, 3328), BF16),
            dma((9,)),
            vmem((2, 80, 128), BF16),
            vmem((2, 8, 80, 128), BF16),
            vmem((2, 80, 128), BF16),
            vmem((2, 8, 80, 128), BF16),
            vmem((128, 128), F32),
            vmem((8, 256), F32),
            vmem((8, 8, 256), F32),
            vmem((2, 8, 16, 384), BF16),
            vmem((2, 8, 16, 384), BF16),
            vmem((2, 16, 384), BF16),
            vmem((2, 8, 16, 384), BF16),
            vmem((2, 16, 128), BF16),
            vmem((2, 8, 16, 128), BF16),
            dma((13,)),
            dma((13,)),
        ],
        compiler_params=pltpu.CompilerParams(
            collective_id=0, has_side_effects=True, vmem_limit_bytes=40 * 1024 * 1024
        ),
        name="decode_step",
    )(
        *(pltpu.with_memory_space_constraint(a, pltpu.HBM) for a in (stream_in, queries[:, 0], key_cache[:, 0], value_cache[:, 0], lengths, out_weight,
        norm_gain, gate_weight, up_weight)),
    )
    stream_out = lax.dynamic_slice_in_dim(residual, lax.axis_index("head") * 32, 32, 1)
    return stream_out, hidden


def solution(mesh):
    return jax.shard_map(
        body,
        mesh=mesh,
        in_specs=(
            P(None, "kvp"),
            P(None, "head", None, None),
            P(None, "head", "kvp", None),
            P(None, "head", "kvp", None),
            P(),
            P("head", "kvp"),
            P("kvp"),
            P("kvp", "head"),
            P("kvp", "head"),
        ),
        out_specs=(P(None, ("kvp", "head")), P(None, "head")),
        check_vma=False,
    )
```

time: 53.2 us -> 47.7 us (0.90)
  local copies, waits for them, and re-layouts: 3.98 us -> 1.28 us
  Pallas kernels: 48.4 us -> 45.7 us
    pallas_call x1, Pallas kernels: 48.4 us -> 45.7 us  [body(): pl.pallas_call(kernel, out_shape=(vmem((8, 256), BF16), vmem((8, 3328), B...]
    reshape x1 -> x0, local copies, waits for them, and re-layouts: 1.22 us -> none  [body(): norm_gain.reshape(1, 256)]
    unnamed x1, local copies, waits for them, and re-layouts: 1.43 us -> 0.62 us
    dynamic_slice x1, local copies, waits for them, and re-layouts: 1.32 us -> 0.66 us  [body(): lax.dynamic_slice_in_dim(residual, lax.axis_index('head') * 32, 32, 1)]
where the time goes in v2:
time: 47.7 us; the launch traced here: 47.6 us
  Pallas kernels  45.7 us (96%)
  local copies, waits for them, and re-layouts  1.28 us (3%)
  between operations  0.65 us (1%)
    pallas_call x1, Pallas kernels, body(): pl.pallas_call(kernel, out_shape=(vmem((8, 256), BF16), vmem((8, 3328), B...  45.7 us

profile of v2, /device:TPU:8, one launch (start us, length us, event | category | flops | bytes accessed | tf_op | source)
XLA Modules:
  0.0 47.6 jit_solution(13886472650006936856)
XLA Ops:
  0.6 45.7 %decode_step.1 = (bf16[8,256]{1,0:T(8,128)(2,1)S(1)}, bf16[8,3328]{1,0:T(8,128)(2,1)S(1)}) custom-call(bf16[8,256]{1,0:T(8,128)(2,1)} %stream_hbm.1, bf16[8,16,128]{2,1,0:T(8,128)(2,1)} %bitcast.5, bf16[8,128,128]{2,1,0:T(8,128)(2,1)} %bitcast.3, bf16[8,128,128]{2,1,0:T(8,128)(2,1)} %bitcast.4, s32[8]{0:T(128)} %len_hbm.1, bf16[2048,256]{1,0:T(8,128)(2,1)} %ow_hbm.1, ...), custom_call_target="tpu_custom_call" | custom-call | tf_op jit(solution)/shard_map/decode_step/pallas_call | solution.py:231
  46.3 0.7 %constant_dynamic-slice_fusion = bf16[8,32]{1,0:T(8,128)(2,1)} fusion(bf16[8,256]{1,0:T(8,128)(2,1)S(1)} %get-tuple-element.4, s32[]{:T(128)S(6)} %select_n.3), kind=kLoop, calls=%fused_computation | loop fusion | bytes 1028 | tf_op jit(solution)/shard_map/dynamic_slice | solution.py:271
  47.0 0.6 %copy.12 = bf16[8,3328]{1,0:T(8,128)(2,1)} copy(bf16[8,3328]{1,0:T(8,128)(2,1)S(1)} %get-tuple-element.7) | data formatting | bytes 106496

commit v3 on v2

--- a/solution.py
+++ b/solution.py
@@ -58,6 +58,16 @@
         half = (n + 1) // 2
         return lax.rem(me + jnp.where(lax.rem(n, 2) == 0, 4 + half, 4 - half), 8)
 
+    loads = {}
+    for n, (name, src, dst) in enumerate((
+        ("k", k_hbm, k_ref), ("q", q_hbm, q_ref), ("len", len_hbm, len_ref), ("v", v_hbm, v_ref),
+        ("stream", stream_hbm, stream_ref), ("gain", gain_hbm, gain_ref),
+        ("ow", ow_hbm, ow_ref), ("gw", gw_hbm, gw_ref), ("uw", uw_hbm, uw_ref),
+    )):
+        loads[name] = pltpu.make_async_copy(src, dst, in_sem.at[n])
+        if n < 4:
+            loads[name].start()
+
     barrier = pltpu.get_barrier_semaphore()
 
     @pl.loop(0, 7)
@@ -65,13 +75,7 @@
         for target in (at_z(far_first(z, n)), at_y(far_first(y, n)), at_head(far_first(head, n))):
             pl.semaphore_signal(barrier, inc=1, device_id=target, device_id_type=MESH)
 
-    loads = {}
-    for n, (name, src, dst) in enumerate((
-        ("len", len_hbm, len_ref), ("q", q_hbm, q_ref), ("k", k_hbm, k_ref), ("v", v_hbm, v_ref),
-        ("stream", stream_hbm, stream_ref), ("gain", gain_hbm, gain_ref),
-        ("ow", ow_hbm, ow_ref), ("gw", gw_hbm, gw_ref), ("uw", uw_hbm, uw_ref),
-    )):
-        loads[name] = pltpu.make_async_copy(src, dst, in_sem.at[n])
+    for name in ("stream", "gain", "ow", "gw", "uw"):
         loads[name].start()
 
     def send(phase, f, src_of, recv):
@@ -151,28 +155,35 @@
     arrived(6, h_recv)
     projected = jnp.sum(h_recv[...], axis=0)
     stream_out = (stream_ref[...].astype(F32) + projected).astype(BF16)
-    so_ref[...] = stream_out
     widened = stream_out.astype(F32)
+    so_ref[...] = pltpu.roll(widened, lax.rem(8 - head, 8) * 32, 1)[:, :32].astype(BF16)
     square = jnp.broadcast_to(jnp.sum(widened * widened, axis=1, keepdims=True), (8, 128))
     scaled = (widened * gain_ref[...].astype(F32).reshape(1, 256)).astype(BF16)
 
+    high = square.astype(BF16)
+    squares = jnp.concatenate([square, square - high.astype(F32)], axis=0).astype(BF16)
+    for f in range(2):
+        d1_send[f, 7] = jnp.concatenate([squares, squares], axis=1)
     loads["gw"].wait()
     loads["uw"].wait()
-    high = square.astype(BF16)
-    squares = jnp.concatenate([square, square - high.astype(F32)], axis=0).astype(BF16)
-
-    def eighth(f, k):
-        columns = pl.ds(pl.multiple_of((13 * f + (13 * k) // 8) * 128, 128), 256)
-        gate = jnp.dot(scaled, gw_ref[:, columns], preferred_element_type=F32)
-        up = jnp.dot(scaled, uw_ref[:, columns], preferred_element_type=F32)
-        return jnp.concatenate([jnp.concatenate([gate, up], axis=0).astype(BF16), squares], axis=1)
+
+    def split_squares(f, part):
+        square = part[0:8] + part[8:16]
+        terms = jnp.concatenate([square, square - square.astype(BF16).astype(F32)], axis=0)
+        return jnp.where(place(f) == 7, terms, part).astype(BF16)
 
     @pl.loop(0, 8)
     def _(n):
         for f in range(2):
             me = place(f)
             p = far_first(me, n)
-            d1_send[f, p] = eighth(f, p)
+
+            @pl.when(p < 7)
+            def _():
+                columns = pl.ds(pl.multiple_of((13 * f + jnp.minimum(2 * p, 11)) * 128, 128), 256)
+                gate = jnp.dot(scaled, gw_ref[:, columns], preferred_element_type=F32)
+                up = jnp.dot(scaled, uw_ref[:, columns], preferred_element_type=F32)
+                d1_send[f, p] = jnp.concatenate([gate, up], axis=0).astype(BF16)
 
             @pl.when(n < 7)
             def _():
@@ -185,33 +196,28 @@
     def _(f):
         d1_recv[f, place(f)] = d1_send[f, place(f)]
         arrived(7 + f, d1_recv.at[f])
-        part = jnp.sum(d1_recv[f].astype(F32), axis=0)
-        square = part[0:8, 256:] + part[8:16, 256:]
-        rest = square - square.astype(BF16).astype(F32)
-        part = jnp.concatenate([part[:, :256], jnp.concatenate([square, rest], axis=0)], axis=1)
-        d2_send[f] = part.astype(BF16)
+        d2_send[f] = split_squares(f, jnp.sum(d1_recv[f].astype(F32), axis=0))
         send(9 + f, 1 - f, lambda p: d2_send.at[f], d2_recv.at[f])
         d2_recv[f, place(1 - f)] = d2_send[f]
 
     @pl.loop(0, 2)
     def _(f):
         arrived(9 + f, d2_recv.at[f])
-        part = jnp.sum(d2_recv[f].astype(F32), axis=0)
-        square = part[0:8, 256:] + part[8:16, 256:]
-        inverse = lax.rsqrt(square / D + epsilon)
-        inverse = jnp.concatenate([inverse, inverse], axis=1)
-        gate, up = part[0:8, :256] * inverse, part[8:16, :256] * inverse
-        hidden = gate / (1.0 + jnp.exp(-gate)) * up
-        d3_send[f] = jnp.concatenate([hidden[:, :128], hidden[:, 128:]], axis=0).astype(BF16)
+        d3_send[f] = split_squares(f, jnp.sum(d2_recv[f].astype(F32), axis=0))
         send(11 + f, f, lambda p: d3_send.at[f], d3_recv.at[f])
         d3_recv[f, place(f)] = d3_send[f]
 
     for f in range(2):
         arrived(11 + f, d3_recv.at[f])
+    square = d3_recv[0, 7, :, 0:128].astype(F32)
+    inverse = lax.rsqrt((square[0:8] + square[8:16]) / D + epsilon)
+    for f in range(2):
         for t in range(13):
-            k = max(k for k in range(8) if 13 * k // 8 <= t)
-            half = t - 13 * k // 8
-            hid_ref[:, (13 * f + t) * 128 : (13 * f + t + 1) * 128] = d3_recv[f, k, 8 * half : 8 * half + 8, :]
+            k = min(t // 2, 6)
+            at_column = (t - min(2 * k, 11)) * 128
+            both = d3_recv[f, k, :, at_column : at_column + 128].astype(F32)
+            gate, up = both[0:8] * inverse, both[8:16] * inverse
+            hid_ref[:, (13 * f + t) * 128 : (13 * f + t + 1) * 128] = (gate / (1.0 + jnp.exp(-gate)) * up).astype(BF16)
 
     for f in range(2):
         for phase, buffer in (
@@ -226,11 +232,19 @@
     pltpu.make_async_copy(seven, seven, send_sem.at[6]).wait()
 
 
+def put(so_ref, hid_ref, so_out, hid_out, sem):
+    copies = [pltpu.make_async_copy(so_ref, so_out, sem.at[0]), pltpu.make_async_copy(hid_ref, hid_out, sem.at[1])]
+    for copy in copies:
+        copy.start()
+    for copy in copies:
+        copy.wait()
+
+
 def body(stream_in, queries, key_cache, value_cache, lengths, out_weight, norm_gain, gate_weight, up_weight):
     vmem, dma = pltpu.VMEM, pltpu.SemaphoreType.DMA
     residual, hidden = pl.pallas_call(
         kernel,
-        out_shape=(vmem((8, 256), BF16), vmem((8, 3328), BF16)),
+        out_shape=(vmem((8, 32), BF16), vmem((8, 3328), BF16)),
         in_specs=[pl.BlockSpec(memory_space=pl.ANY)] * 9,
         out_specs=(pl.BlockSpec(memory_space=vmem), pl.BlockSpec(memory_space=vmem)),
         scratch_shapes=[
@@ -251,12 +265,12 @@
             vmem((128, 128), F32),
             vmem((8, 256), F32),
             vmem((8, 8, 256), F32),
-            vmem((2, 8, 16, 384), BF16),
-            vmem((2, 8, 16, 384), BF16),
-            vmem((2, 16, 384), BF16),
-            vmem((2, 8, 16, 384), BF16),
-            vmem((2, 16, 128), BF16),
-            vmem((2, 8, 16, 128), BF16),
+            vmem((2, 8, 16, 256), BF16),
+            vmem((2, 8, 16, 256), BF16),
+            vmem((2, 16, 256), BF16),
+            vmem((2, 8, 16, 256), BF16),
+            vmem((2, 16, 256), BF16),
+            vmem((2, 8, 16, 256), BF16),
             dma((13,)),
             dma((13,)),
         ],
@@ -268,8 +282,14 @@
         *(pltpu.with_memory_space_constraint(a, pltpu.HBM) for a in (stream_in, queries[:, 0], key_cache[:, 0], value_cache[:, 0], lengths, out_weight,
         norm_gain, gate_weight, up_weight)),
     )
-    stream_out = lax.dynamic_slice_in_dim(residual, lax.axis_index("head") * 32, 32, 1)
-    return stream_out, hidden
+    return pl.pallas_call(
+        put,
+        out_shape=(pltpu.HBM((8, 32), BF16), pltpu.HBM((8, 3328), BF16)),
+        in_specs=[pl.BlockSpec(memory_space=pl.ANY)] * 2,
+        out_specs=(pl.BlockSpec(memory_space=pl.ANY), pl.BlockSpec(memory_space=pl.ANY)),
+        scratch_shapes=[dma((2,))],
+        name="put",
+    )(*(pltpu.with_memory_space_constraint(a, pltpu.VMEM) for a in (residual, hidden)))
 
 
 def solution(mesh):

time: 47.7 us -> 46.7 us (0.979)
  local copies, waits for them, and re-layouts: 1.28 us -> 0 us
    dynamic_slice x1 -> x0, local copies, waits for them, and re-layouts: 0.66 us -> none  [body(): lax.dynamic_slice_in_dim(residual, lax.axis_index('head') * 32, 32, 1)]
    unnamed x1 -> x0, local copies, waits for them, and re-layouts: 0.62 us -> none
    pallas_call x1 -> x2, Pallas kernels: 45.7 us -> 45.9 us  [the longest x1 45.3 us: body(): pl.pallas_call(kernel, out_shape=(vmem((8, 32), BF16), vmem((8, 3328), BF...]
where the time goes in v3:
time: 46.7 us; the launch traced here: 46.6 us
  Pallas kernels  45.9 us (98%)
  between operations  0.64 us (1%)
    pallas_call x1, Pallas kernels, body(): pl.pallas_call(kernel, out_shape=(vmem((8, 32), BF16), vmem((8, 3328), BF...  45.3 us

profile of v3, /device:TPU:8, one launch (start us, length us, event | category | flops | bytes accessed | tf_op | source)
XLA Modules:
  0.0 46.6 jit_solution(6410892319716391187)
XLA Ops:
  0.6 45.3 %decode_step.1 = (bf16[8,32]{1,0:T(8,128)(2,1)S(1)}, bf16[8,3328]{1,0:T(8,128)(2,1)S(1)}) custom-call(bf16[8,256]{1,0:T(8,128)(2,1)} %stream_hbm.1, bf16[8,16,128]{2,1,0:T(8,128)(2,1)} %bitcast.5, bf16[8,128,128]{2,1,0:T(8,128)(2,1)} %bitcast.3, bf16[8,128,128]{2,1,0:T(8,128)(2,1)} %bitcast.4, s32[8]{0:T(128)} %len_hbm.1, bf16[2048,256]{1,0:T(8,128)(2,1)} %ow_hbm.1, ...), custom_call_target="tpu_custom_call" | custom-call | tf_op jit(solution)/shard_map/decode_step/pallas_call | solution.py:245
  45.9 0.6 %put.1 = (bf16[8,32]{1,0:T(8,128)(2,1)}, bf16[8,3328]{1,0:T(8,128)(2,1)}) custom-call(bf16[8,32]{1,0:T(8,128)(2,1)S(1)} %get-tuple-element.4.so_ref, bf16[8,3328]{1,0:T(8,128)(2,1)S(1)} %get-tuple-element.5.hid_ref), custom_call_target="tpu_custom_call" | custom-call | tf_op jit(solution)/shard_map/put/pallas_call | solution.py:285

commit v4 on v3

--- a/solution.py
+++ b/solution.py
@@ -14,18 +14,22 @@
 
 
 def merge(parts):
-    stats = parts[:, 64:80, :].astype(F32)
+    stats = parts[:, 8].astype(F32)
     shift = jnp.max(stats, axis=0)
     scale = jnp.exp(stats - shift[None])
-    weight = jnp.sum(scale * pltpu.roll(stats.reshape(128, 128), 112, 1).reshape(8, 16, 128), axis=0)
+    weight = jnp.sum(scale * pltpu.roll(stats.reshape(64, 128), 112, 1).reshape(8, 8, 128), axis=0)
     totals = []
-    for s in range(4):
+    for b in range(8):
         total = None
         for k in range(8):
-            term = scale[k, :, 32 * s : 32 * s + 1] * parts[k, 16 * s : 16 * s + 16, :].astype(F32)
+            term = scale[k, :, stats_lane(b) : stats_lane(b) + 1] * parts[k, b].astype(F32)
             total = term if total is None else total + term
         totals.append(total)
     return totals, shift, weight
+
+
+def stats_lane(b):
+    return 32 * (b // 2) + 8 * (b % 2)
 
 
 def kernel(
@@ -94,10 +98,10 @@
 
     for name in ("len", "q", "k", "v"):
         loads[name].wait()
-    lane = lax.broadcasted_iota(jnp.int32, (16, 128), 1)
-    position = kvp * 128 + lane
-    for f in range(2):
-        stats = jnp.zeros((16, 128), F32)
+    position = kvp * 128 + lax.broadcasted_iota(jnp.int32, (16, 128), 1)
+    lane = lax.broadcasted_iota(jnp.int32, (8, 128), 1)
+    for f in range(2):
+        stats = jnp.zeros((8, 128), F32)
         for s in range(4):
             score = lax.dot_general(
                 q_ref[4 * f + s], k_ref[4 * f + s], (((1,), (1,)), ((), ())), preferred_element_type=F32
@@ -108,9 +112,12 @@
             weight = jnp.where(inside, jnp.exp(score - top), 0.0).astype(BF16)
             weight_sum = jnp.sum(weight.astype(F32), axis=1, keepdims=True)
             total = jnp.dot(weight, v_ref[4 * f + s], preferred_element_type=F32)
-            a1_send[f, 16 * s : 16 * s + 16] = total.astype(BF16)
-            stats = jnp.where(lane // 16 == 2 * s, top, jnp.where(lane // 16 == 2 * s + 1, weight_sum, stats))
-        a1_send[f, 64:80] = stats.astype(BF16)
+            for i in range(2):
+                part = slice(8 * i, 8 * i + 8)
+                a1_send[f, 2 * s + i] = total[part].astype(BF16)
+                stats = jnp.where(lane // 8 == 4 * s + i, top[part], stats)
+                stats = jnp.where(lane // 8 == 4 * s + 2 + i, weight_sum[part], stats)
+        a1_send[f, 8] = stats.astype(BF16)
 
     pl.semaphore_wait(barrier, 21)
 
@@ -124,9 +131,9 @@
     def _(f):
         arrived(f, a1_recv.at[f])
         totals, shift, weight = merge(a1_recv[f])
-        for s in range(4):
-            a2_send[f, 16 * s : 16 * s + 16] = totals[s].astype(BF16)
-        a2_send[f, 64:80] = jnp.where(lax.rem(lane // 16, 2) == 0, shift, pltpu.roll(weight, 16, 1)).astype(BF16)
+        for b in range(8):
+            a2_send[f, b] = totals[b].astype(BF16)
+        a2_send[f, 8] = jnp.where(lax.rem(lane // 16, 2) == 0, shift, pltpu.roll(weight, 16, 1)).astype(BF16)
         send(2 + f, 1 - f, lambda p: a2_send.at[f], a2_recv.at[f])
         a2_recv[f, place(1 - f)] = a2_send[f]
 
@@ -135,8 +142,8 @@
         arrived(2 + f, a2_recv.at[f])
         totals, _, weight = merge(a2_recv[f])
         inverse = 1.0 / weight
-        for s in range(4):
-            rows[pl.ds(64 * f + 16 * s, 16)] = totals[s] * inverse[:, 32 * s : 32 * s + 1]
+        for b in range(8):
+            rows[pl.ds(64 * f + 8 * b, 8)] = totals[b] * inverse[:, stats_lane(b) : stats_lane(b) + 1]
 
     loads["ow"].wait()
     loads["stream"].wait()
@@ -258,10 +265,10 @@
             vmem((256, 3328), BF16),
             vmem((256, 3328), BF16),
             dma((9,)),
-            vmem((2, 80, 128), BF16),
-            vmem((2, 8, 80, 128), BF16),
-            vmem((2, 80, 128), BF16),
-            vmem((2, 8, 80, 128), BF16),
+            vmem((2, 9, 8, 128), BF16),
+            vmem((2, 8, 9, 8, 128), BF16),
+            vmem((2, 9, 8, 128), BF16),
+            vmem((2, 8, 9, 8, 128), BF16),
             vmem((128, 128), F32),
             vmem((8, 256), F32),
             vmem((8, 8, 256), F32),

time: 46.7 us -> 45.8 us (0.981)
  Pallas kernels: 45.9 us -> 45 us
    pallas_call x1, Pallas kernels: 45.3 us -> 44.4 us  [body(): pl.pallas_call(kernel, out_shape=(vmem((8, 32), BF16), vmem((8, 3328), BF...]
where the time goes in v4:
time: 45.8 us; the launch traced here: 45.7 us
  Pallas kernels  45 us (98%)
  between operations  0.64 us (1%)
    pallas_call x1, Pallas kernels, body(): pl.pallas_call(kernel, out_shape=(vmem((8, 32), BF16), vmem((8, 3328), BF...  44.4 us

profile of v4, /device:TPU:8, one launch (start us, length us, event | category | flops | bytes accessed | tf_op | source)
XLA Modules:
  0.0 45.7 jit_solution(451682690553566822)
XLA Ops:
  0.6 44.4 %decode_step.1 = (bf16[8,32]{1,0:T(8,128)(2,1)S(1)}, bf16[8,3328]{1,0:T(8,128)(2,1)S(1)}) custom-call(bf16[8,256]{1,0:T(8,128)(2,1)} %stream_hbm.1, bf16[8,16,128]{2,1,0:T(8,128)(2,1)} %bitcast.5, bf16[8,128,128]{2,1,0:T(8,128)(2,1)} %bitcast.3, bf16[8,128,128]{2,1,0:T(8,128)(2,1)} %bitcast.4, s32[8]{0:T(128)} %len_hbm.1, bf16[2048,256]{1,0:T(8,128)(2,1)} %ow_hbm.1, ...), custom_call_target="tpu_custom_call" | custom-call | tf_op jit(solution)/shard_map/decode_step/pallas_call | solution.py:252
  45.0 0.6 %put.1 = (bf16[8,32]{1,0:T(8,128)(2,1)}, bf16[8,3328]{1,0:T(8,128)(2,1)}) custom-call(bf16[8,32]{1,0:T(8,128)(2,1)S(1)} %get-tuple-element.4.so_ref, bf16[8,3328]{1,0:T(8,128)(2,1)S(1)} %get-tuple-element.5.hid_ref), custom_call_target="tpu_custom_call" | custom-call | tf_op jit(solution)/shard_map/put/pallas_call | solution.py:292

commit v5 on v4

--- a/solution.py
+++ b/solution.py
@@ -211,20 +211,17 @@
     def _(f):
         arrived(9 + f, d2_recv.at[f])
         d3_send[f] = split_squares(f, jnp.sum(d2_recv[f].astype(F32), axis=0))
-        send(11 + f, f, lambda p: d3_send.at[f], d3_recv.at[f])
+        me = place(f)
+
+        @pl.loop(0, 7)
+        def _(n):
+            p = n + jnp.where(n >= me, 1, 0)
+            pltpu.make_async_remote_copy(
+                d3_send.at[f], d3_recv.at[f, me], send_sem.at[11 + f], recv_sem.at[11 + f],
+                device_id=at(f, p), device_id_type=MESH,
+            ).start()
+
         d3_recv[f, place(f)] = d3_send[f]
-
-    for f in range(2):
-        arrived(11 + f, d3_recv.at[f])
-    square = d3_recv[0, 7, :, 0:128].astype(F32)
-    inverse = lax.rsqrt((square[0:8] + square[8:16]) / D + epsilon)
-    for f in range(2):
-        for t in range(13):
-            k = min(t // 2, 6)
-            at_column = (t - min(2 * k, 11)) * 128
-            both = d3_recv[f, k, :, at_column : at_column + 128].astype(F32)
-            gate, up = both[0:8] * inverse, both[8:16] * inverse
-            hid_ref[:, (13 * f + t) * 128 : (13 * f + t + 1) * 128] = (gate / (1.0 + jnp.exp(-gate)) * up).astype(BF16)
 
     for f in range(2):
         for phase, buffer in (
@@ -237,6 +234,18 @@
             pltpu.make_async_copy(buffer, buffer, send_sem.at[phase]).wait()
     seven = h_recv.at[pl.ds(0, 7)]
     pltpu.make_async_copy(seven, seven, send_sem.at[6]).wait()
+
+    for f in range(2):
+        arrived(11 + f, d3_recv.at[f])
+        if f == 0:
+            square = d3_recv[0, 7, :, 0:128].astype(F32)
+            inverse = lax.rsqrt((square[0:8] + square[8:16]) / D + epsilon)
+        for t in range(13):
+            k = min(t // 2, 6)
+            at_column = (t - min(2 * k, 11)) * 128
+            both = d3_recv[f, k, :, at_column : at_column + 128].astype(F32)
+            gate, up = both[0:8] * inverse, both[8:16] * inverse
+            hid_ref[:, (13 * f + t) * 128 : (13 * f + t + 1) * 128] = (gate / (1.0 + jnp.exp(-gate)) * up).astype(BF16)
 
 
 def put(so_ref, hid_ref, so_out, hid_out, sem):

time: 45.8 us -> 45.8 us (level)
  no operation moved by 1% of the time
where the time goes in v5:
time: 45.8 us; the launch traced here: 45.6 us
  Pallas kernels  45 us (98%)
  between operations  0.64 us (1%)
    pallas_call x1, Pallas kernels, body(): pl.pallas_call(kernel, out_shape=(vmem((8, 32), BF16), vmem((8, 3328), BF...  44.4 us

profile of v5, /device:TPU:8, one launch (start us, length us, event | category | flops | bytes accessed | tf_op | source)
XLA Modules:
  0.0 45.6 jit_solution(11476123079983798722)
XLA Ops:
  0.6 44.4 %decode_step.1 = (bf16[8,32]{1,0:T(8,128)(2,1)S(1)}, bf16[8,3328]{1,0:T(8,128)(2,1)S(1)}) custom-call(bf16[8,256]{1,0:T(8,128)(2,1)} %stream_hbm.1, bf16[8,16,128]{2,1,0:T(8,128)(2,1)} %bitcast.5, bf16[8,128,128]{2,1,0:T(8,128)(2,1)} %bitcast.3, bf16[8,128,128]{2,1,0:T(8,128)(2,1)} %bitcast.4, s32[8]{0:T(128)} %len_hbm.1, bf16[2048,256]{1,0:T(8,128)(2,1)} %ow_hbm.1, ...), custom_call_target="tpu_custom_call" | custom-call | tf_op jit(solution)/shard_map/decode_step/pallas_call | solution.py:261
  45.0 0.6 %put.1 = (bf16[8,32]{1,0:T(8,128)(2,1)}, bf16[8,3328]{1,0:T(8,128)(2,1)}) custom-call(bf16[8,32]{1,0:T(8,128)(2,1)S(1)} %get-tuple-element.4.so_ref, bf16[8,3328]{1,0:T(8,128)(2,1)S(1)} %get-tuple-element.5.hid_ref), custom_call_target="tpu_custom_call" | custom-call | tf_op jit(solution)/shard_map/put/pallas_call | solution.py:301
